TPU v7x, 32 devices: a whole 2x2x4 slice. The times are simulated.
32 devices in a mesh: dp: 4 (over x, core), seq: 8 (over z, y).
Axes of the slice: x: 2, y: 2, z: 4, core: 2. Of those that a mesh axis runs over, the one named last changes fastest.
Arguments:
- inputs: bfloat16 [4, 4096, 768], P('dp', 'seq'), may hold values from -6 to 6
- block_mix: bfloat16 [8, 512, 512], P('seq'), may hold values from -0.25 to 0.25
- cross_mix: bfloat16 [512, 8, 8], P('seq'), may hold values from -2 to 2
- cotangent: bfloat16 [4, 4096, 768], P('dp', 'seq'), may hold values from -0.59765625 to 0.59765625
Outputs:
- output: bfloat16 [4, 4096, 768], P('dp', 'seq')
- input_grad: bfloat16 [4, 4096, 768], P('dp', 'seq')
- block_grad: bfloat16 [8, 512, 512], P('seq')
- cross_grad: bfloat16 [512, 8, 8], P('seq')
All inputs are finite; a program needn't handle non-finite values.
Results may differ from a plain program's by a relative error of at most 0.012.
Values may be sent and summed in bfloat16 or wider, within the bound.
A program may use at most 64 MiB of HBM per device.

v0:
```python
import jax
import jax.numpy as jnp
from jax import lax
from jax.sharding import PartitionSpec as P


def local(inputs, block_mix, cross_mix, cotangent):
    h = jnp.einsum("bsr,brc->bsc", block_mix, inputs, preferred_element_type=jnp.float32).astype(
        jnp.bfloat16
    )
    gate = jax.nn.sigmoid(inputs.astype(jnp.float32))
    h_cols = lax.all_to_all(h, "seq", split_axis=1, concat_axis=0, tiled=True)
    z_cols = jnp.einsum(
        "rab,brc->arc", cross_mix, h_cols, preferred_element_type=jnp.float32
    ).astype(jnp.bfloat16)
    z = lax.all_to_all(z_cols, "seq", split_axis=0, concat_axis=1, tiled=True)
    dz = (cotangent.astype(jnp.float32) * gate).astype(jnp.bfloat16)
    dz_cols = lax.all_to_all(dz, "seq", split_axis=1, concat_axis=0, tiled=True)
    dh_cols = jnp.einsum(
        "rab,arc->brc", cross_mix, dz_cols, preferred_element_type=jnp.float32
    ).astype(jnp.bfloat16)
    cross_part = jnp.einsum("arc,brc->rab", dz_cols, h_cols, preferred_element_type=jnp.float32)
    dh = lax.all_to_all(dh_cols, "seq", split_axis=0, concat_axis=1, tiled=True)
    dv = jnp.einsum("bsr,bsc->brc", block_mix, dh, preferred_element_type=jnp.float32)
    block_part = jnp.einsum("bsc,brc->bsr", dh, inputs, preferred_element_type=jnp.float32)
    block_sum, cross_sum = (
        lax.psum(block_part.astype(jnp.bfloat16), "dp").astype(jnp.float32),
        lax.psum(cross_part.astype(jnp.bfloat16), "dp").astype(jnp.float32),
    )
    zf = z.astype(jnp.float32)
    output = (inputs.astype(jnp.float32) + zf * gate).astype(jnp.bfloat16)
    input_grad = (cotangent.astype(jnp.float32) * (1.0 + zf * gate * (1.0 - gate)) + dv).astype(
        jnp.bfloat16
    )
    return (output, input_grad, block_sum.astype(jnp.bfloat16), cross_sum.astype(jnp.bfloat16))


def solution(mesh):
    placed = (
        P("dp", "seq", None),
        P("seq", None, None),
        P("seq", None, None),
        P("dp", "seq", None),
    )
    return jax.shard_map(
        local,
        mesh=mesh,
        in_specs=placed,
        out_specs=(
            P("dp", "seq", None),
            P("dp", "seq", None),
            P("seq", None, None),
            P("seq", None, None),
        ),
        check_vma=False,
    )
```

profile of v0, /device:TPU:0, one launch (start us, length us, event | category | flops | bytes accessed | tf_op | source)
XLA Modules:
  0.0 190.0 jit_solution(17759699037681168629)
XLA Ops:
  7.2 1.0 copy-done
  8.2 1.7 fusion.9
  9.9 1.2 copy.73
  11.7 5.4 %reduce = bf16[512,768]{1,0:T(8,128)(2,1)S(1)} reduce(bf16[512,1,768]{2,1,0:T(2,128)(2,1)S(1)} %bitcast.39, bf16[]{:T(256)} %broadcast.12), dimensions={1}, to_apply=%bitcast.37.reduce_sub_computation | reduce | bytes 1572866
  17.1 1.1 reshape.57
  18.2 7.3 %all-to-all-start = ((bf16[8,2,24576]{2,1,0:T(2,128)(2,1)}), bf16[8,2,24576]{2,1,0:T(2,128)(2,1)S(1)}, u32[]{:S(2)}, u32[]{:S(2)}) async-start(bf16[8,2,24576]{2,1,0:T(2,128)(2,1)} %reshape.57), calls=%async_computation | async-start | bytes 1572864 | tf_op jit(solution)/shard_map/all_to_all | solution.py:12
  25.6 20.0 %all-to-all-done = bf16[8,2,24576]{2,1,0:T(2,128)(2,1)S(1)} async-done(((bf16[8,2,24576]{2,1,0:T(2,128)(2,1)}), bf16[8,2,24576]{2,1,0:T(2,128)(2,1)S(1)}, u32[]{:S(2)}, u32[]{:S(2)}) %all-to-all-start) | async-done | bytes 786464 | tf_op jit(solution)/shard_map/all_to_all | solution.py:12
  46.6 0.9 copy-done.4
  48.0 1.0 copy.50
  49.1 3.9 %all-to-all-start.1 = ((bf16[8,64,768]{2,1,0:T(8,128)(2,1)}), bf16[8,64,768]{2,1,0:T(8,128)(2,1)S(1)}, u32[]{:S(2)}, u32[]{:S(2)}) async-start(bf16[8,64,768]{2,1,0:T(8,128)(2,1)} %copy.50), calls=%async_computation.1 | async-start | bytes 1572864 | tf_op jit(solution)/shard_map/all_to_all | solution.py:16
  52.9 1.4 copy.46
  54.4 1.2 copy.52
  55.5 17.6 %all-to-all-done.1 = bf16[8,64,768]{2,1,0:T(8,128)(2,1)S(1)} async-done(((bf16[8,64,768]{2,1,0:T(8,128)(2,1)}), bf16[8,64,768]{2,1,0:T(8,128)(2,1)S(1)}, u32[]{:S(2)}, u32[]{:S(2)}) %all-to-all-start.1) | async-done | bytes 786464 | tf_op jit(solution)/shard_map/all_to_all | solution.py:16
  74.0 1.2 bitcast_convert_fusion
  75.2 1.6 copy.51
  76.8 3.4 %fusion.6 = (bf16[1,512,768]{1,2,0:T(8,128)(2,1)}, bf16[1,512,768]{1,2,0:T(8,128)(2,1)}) fusion(bf16[1,512,768]{1,2,0:T(8,128)(2,1)} %copy.52, bf16[1,512,768]{1,2,0:T(8,128)(2,1)S(1)} %copy.46, f32[1,512,768]{1,2,0:T(8,128)} %copy.51), kind=kLoop, calls=%fused_computation.10 | loop fusion | flops 3932160 | bytes 4718592 | tf_op jit(solution)/shard_map/convert_element_type | solution.py:17
  80.2 3.7 %copy.53 = bf16[1,512,768]{2,0,1:T(2,128)(2,1)S(1)} copy(bf16[1,512,768]{1,2,0:T(8,128)(2,1)} %get-tuple-element.20) | data formatting | bytes 1572864 | tf_op jit(solution)/shard_map/convert_element_type | solution.py:17
  84.0 6.3 %reduce.1 = bf16[512,768]{1,0:T(8,128)(2,1)} reduce(bf16[512,1,768]{2,1,0:T(2,128)(2,1)S(1)} %bitcast.40, bf16[]{:T(256)} %broadcast.12), dimensions={1}, to_apply=%bitcast.30.reduce_sub_computation | reduce | bytes 1572866
  90.3 2.2 %reshape.59 = bf16[8,2,24576]{2,1,0:T(2,128)(2,1)S(1)} reshape(bf16[512,768]{1,0:T(8,128)(2,1)} %reduce.1) | data formatting | bytes 1572864
  92.5 23.8 %all_to_all.42 = bf16[8,2,24576]{2,1,0:T(2,128)(2,1)} all-to-all(bf16[8,2,24576]{2,1,0:T(2,128)(2,1)S(1)} %reshape.59), channel_id=1, replica_groups=mesh['dp'=4,'seq'=8] {'seq'}, dimensions={0} | all-to-all | bytes 1572864 | tf_op jit(solution)/shard_map/all_to_all | solution.py:18
  116.3 4.1 %reshape.60 = bf16[512,1,768]{2,1,0:T(2,128)(2,1)S(1)} reshape(bf16[8,2,24576]{2,1,0:T(2,128)(2,1)} %all_to_all.42) | data formatting | bytes 1572864
  121.4 1.0 copy.56
  122.5 4.3 %all-to-all-start.3 = ((bf16[8,64,768]{2,1,0:T(8,128)(2,1)}), bf16[8,64,768]{2,1,0:T(8,128)(2,1)}, u32[]{:S(2)}, u32[]{:S(2)}) async-start(bf16[8,64,768]{2,1,0:T(8,128)(2,1)} %copy.56), calls=%async_computation.3 | async-start | bytes 1572864 | tf_op jit(solution)/shard_map/all_to_all | solution.py:23
  126.9 1.2 copy.59
  128.0 2.1 %convolution_convert_fusion.4 = bf16[64,8,8]{2,1,0:T(8,128)(2,1)S(1)} fusion(bf16[8,64,768]{2,1,0:T(8,128)(2,1)} %bitcast.47, bf16[8,64,768]{2,1,0:T(8,128)(2,1)S(1)} %bitcast.45), kind=kOutput, calls=%fused_computation.19 | convolution fusion | flops 6295552 | bytes 1581056 | tf_op jit(solution)/shard_map/arc,brc->rab/dot_general | solution.py:22
  130.1 12.4 %psum.15 = bf16[64,8,8]{2,1,0:T(8,128)(2,1)S(1)} all-reduce(bf16[64,8,8]{2,1,0:T(8,128)(2,1)S(1)} %convolution_convert_fusion.4), channel_id=1, replica_groups=mesh['dp'=4,'seq'=8] {'dp'}, use_global_device_ids=true, to_apply=%region_1.0 | all-reduce | flops 4096 | bytes 16384 | tf_op jit(solution)/shard_map/psum | solution.py:28
  143.2 3.0 %all-to-all-done.3 = bf16[8,64,768]{2,1,0:T(8,128)(2,1)} async-done(((bf16[8,64,768]{2,1,0:T(8,128)(2,1)}), bf16[8,64,768]{2,1,0:T(8,128)(2,1)}, u32[]{:S(2)}, u32[]{:S(2)}) %all-to-all-start.3) | async-done | bytes 786464 | tf_op jit(solution)/shard_map/all_to_all | solution.py:23
  146.2 2.8 %fusion.10 = bf16[1,512,512]{2,1,0:T(8,128)(2,1)} fusion(bf16[512,768]{1,0:T(8,128)(2,1)} %bitcast.6, bf16[1,512,768]{2,1,0:T(8,128)(2,1)} %param.4), kind=kOutput, calls=%fused_computation.18 | convolution fusion | flops 402915328 | bytes 2097152 | tf_op jit(solution)/shard_map/bsc,brc->bsr/dot_general | solution.py:25
  149.0 3.2 %fusion.5 = bf16[1,512,768]{1,2,0:T(8,128)(2,1)} fusion(bf16[1,512,768]{1,2,0:T(8,128)(2,1)} %copy.52, bf16[512,768]{1,0:T(8,128)(2,1)} %bitcast.6, f32[1,512,768]{1,2,0:T(8,128)S(1)} %copy-done.1, bf16[1,512,512]{2,1,0:T(8,128)(2,1)S(1)} %copy-done, bf16[1,512,768]{1,2,0:T(8,128)(2,1)S(1)} %copy.46), kind=kOutput, calls=%fused_computation.9 | convolution fusion | flops 407371776 | bytes 5242880 | tf_op jit(solution)/shard_map/bsr,bsc->brc/dot_general | solution.py:24
  152.3 2.3 %copy.60 = bf16[1,512,768]{2,1,0:T(8,128)(2,1)} copy(bf16[1,512,768]{1,2,0:T(8,128)(2,1)} %fusion.5) | data formatting | bytes 1572864
  154.6 26.8 %all-reduce.2.cloned.1.call-done = bf16[1,512,512]{2,1,0:T(8,128)(2,1)} async-done(((bf16[1,512,512]{2,1,0:T(8,128)(2,1)}), bf16[1,512,512]{2,1,0:T(8,128)(2,1)}) %all-reduce.2.cloned.1.call-update) | async-done | bytes 524304 | tf_op jit(solution)/shard_map/psum | solution.py:27
  181.3 1.9 copy.75
  (26 shorter events, 4.9 us)
Async XLA Ops:
  7.2 1.0 copy-start
  17.1 8.4 %copy-start.8 = (bf16[64,8,8]{0,2,1:T(8,128)(2,1)S(1)}, bf16[64,8,8]{0,2,1:T(8,128)(2,1)}, u32[]{:S(2)}) copy-start(bf16[64,8,8]{0,2,1:T(8,128)(2,1)} %param.6) | copy-start | bytes 24580
  18.2 27.5 %all-to-all-start = ((bf16[8,2,24576]{2,1,0:T(2,128)(2,1)}), bf16[8,2,24576]{2,1,0:T(2,128)(2,1)S(1)}, u32[]{:S(2)}, u32[]{:S(2)}) async-start(bf16[8,2,24576]{2,1,0:T(2,128)(2,1)} %reshape.57), calls=%async_computation | async-start | bytes 1572864 | tf_op jit(solution)/shard_map/all_to_all | solution.py:12
  46.6 0.9 copy-start.4
  49.1 5.3 %copy-start.7 = (bf16[1,512,768]{2,1,0:T(8,128)(2,1)S(1)}, bf16[1,512,768]{2,1,0:T(8,128)(2,1)}, u32[]{:S(2)}) copy-start(bf16[1,512,768]{2,1,0:T(8,128)(2,1)} %param.7) | copy-start | bytes 2359300
  49.1 24.0 %all-to-all-start.1 = ((bf16[8,64,768]{2,1,0:T(8,128)(2,1)}), bf16[8,64,768]{2,1,0:T(8,128)(2,1)S(1)}, u32[]{:S(2)}, u32[]{:S(2)}) async-start(bf16[8,64,768]{2,1,0:T(8,128)(2,1)} %copy.50), calls=%async_computation.1 | async-start | bytes 1572864 | tf_op jit(solution)/shard_map/all_to_all | solution.py:16
  73.1 0.9 copy-start.3
  120.5 0.9 copy-start.6
  121.4 5.4 %copy-start.2 = (bf16[1,512,768]{1,2,0:T(8,128)(2,1)S(1)}, bf16[1,512,768]{1,2,0:T(8,128)(2,1)}, u32[]{:S(2)}) copy-start(bf16[1,512,768]{1,2,0:T(8,128)(2,1)} %get-tuple-element.21) | copy-start | bytes 2359300
  122.5 5.6 %copy-start.5 = (bf16[1,512,768]{2,1,0:T(8,128)(2,1)S(1)}, bf16[1,512,768]{2,1,0:T(8,128)(2,1)}, u32[]{:S(2)}) copy-start(bf16[1,512,768]{2,1,0:T(8,128)(2,1)} %copy-done.4) | copy-start | bytes 2359300
  122.5 23.8 %all-to-all-start.3 = ((bf16[8,64,768]{2,1,0:T(8,128)(2,1)}), bf16[8,64,768]{2,1,0:T(8,128)(2,1)}, u32[]{:S(2)}, u32[]{:S(2)}) async-start(bf16[8,64,768]{2,1,0:T(8,128)(2,1)} %copy.56), calls=%async_computation.3 | async-start | bytes 1572864 | tf_op jit(solution)/shard_map/all_to_all | solution.py:23
  126.8 54.5 %all-reduce.2.cloned.1.call-start = ((), (), s32[]{:S(2)}) async-start(), calls=%async_computation.4 | async-start | bytes 1048576 | tf_op jit(solution)/shard_map/psum | solution.py:27
  142.5 6.5 %copy-start.1 = (f32[1,512,768]{1,2,0:T(8,128)S(1)}, f32[1,512,768]{1,2,0:T(8,128)}, u32[]{:S(2)}) copy-start(f32[1,512,768]{1,2,0:T(8,128)} %copy.51) | copy-start | bytes 4718596
Sparse Core Ops, SparseCore 0:
  149.2 32.1 all-reduce.1
where the time goes:
time: 191 us; the launch traced here: 190 us
  waiting for transfers between devices  67.4 us (35%)
  blocking collectives  36.1 us (19%)
  local copies, waits for them, and re-layouts  29.5 us (15%)
  other arithmetic  16.4 us (9%)
  starting transfers between devices  15.5 us (8%)
  between operations  14.2 us (7%)
  matrix products  10.9 us (6%)
    psum x1, waiting for transfers between devices, local(): lax.psum(block_part.astype(jnp.bfloat16), 'dp').astype(jnp.float32)  26.8 us
    all_to_all x1, blocking collectives, local(): dz_cols = lax.all_to_all(dz, 'seq', split_axis=1, concat_axis=0, tiled=True)  23.8 us
    unnamed x32, local copies, waits for them, and re-layouts  20.9 us
    all_to_all x1, waiting for transfers between devices, local(): h_cols = lax.all_to_all(h, 'seq', split_axis=1, concat_axis=0, tiled=True)  20 us
    all_to_all x1, waiting for transfers between devices, local(): z = lax.all_to_all(z_cols, 'seq', split_axis=0, concat_axis=1, tiled=True)  17.6 us
    psum x1, blocking collectives, local(): lax.psum(cross_part.astype(jnp.bfloat16), 'dp').astype(jnp.float32)  12.4 us
    unnamed x2, other arithmetic  11.7 us
    all_to_all x1, starting transfers between devices, local(): h_cols = lax.all_to_all(h, 'seq', split_axis=1, concat_axis=0, tiled=True)  7.28 us
  transfers between devices with their start and end apart: 4, of which 4 were waited for; matrix products, arithmetic and copies ran while one was open for 6% of the time, Pallas kernels for 0%

commit v1 on v0

--- a/solution.py
+++ b/solution.py
@@ -1,10 +1,17 @@
+import functools
+
 import jax
 import jax.numpy as jnp
 from jax import lax
+from jax.experimental import pallas as pl
+from jax.experimental.pallas import tpu as pltpu
 from jax.sharding import PartitionSpec as P
 
-
-def local(inputs, block_mix, cross_mix, cotangent):
+MESH = pl.DeviceIdType.MESH
+BF16, F32 = jnp.bfloat16, jnp.float32
+
+
+def plain(inputs, block_mix, cross_mix, cotangent):
     h = jnp.einsum("bsr,brc->bsc", block_mix, inputs, preferred_element_type=jnp.float32).astype(
         jnp.bfloat16
     )
@@ -35,6 +42,273 @@
     return (output, input_grad, block_sum.astype(jnp.bfloat16), cross_sum.astype(jnp.bfloat16))
 
 
+def mix(
+    nb, dp, rows, group,
+    x_ref, b_ref, w_ref, cot_ref,
+    out_ref, ig_ref, bg_ref, cg_ref,
+    gate, dz, h, dz_in, h_in, dh_out, z_out, dh, z, dv,
+    weight, bpart, brecv, cpart, crecv,
+    send, recv, csend, crecv_sem, rsend, rrecv, gsend, grecv,
+):
+    me, mp = lax.axis_index("seq"), lax.axis_index("dp")
+    side = nb * group
+    groups = rows // group
+    size, chan = x_ref.shape
+    share = size // dp
+    order = sorted(range(1, nb), key=lambda d: abs(d - nb / 2))
+
+    barrier = pltpu.get_barrier_semaphore()
+    for d in range(1, nb):
+        pl.semaphore_signal(
+            barrier, inc=1, device_id={"seq": lax.rem(me + d, nb)}, device_id_type=MESH
+        )
+    for e in range(1, dp):
+        pl.semaphore_signal(
+            barrier, inc=1, device_id={"dp": lax.rem(mp + e, dp)}, device_id_type=MESH
+        )
+
+    def exchange(k, d, src, dst, to, slot):
+        return pltpu.make_async_remote_copy(
+            src_ref=src.at[to],
+            dst_ref=dst.at[slot],
+            send_sem=send.at[k, d],
+            recv_sem=recv.at[k, d],
+            device_id={"seq": to},
+            device_id_type=MESH,
+        )
+
+    def push(k, src, dst):
+        for d in order:
+            exchange(k, d, src, dst, lax.rem(me + d, nb), me).start()
+        dst[me] = src[me]
+
+    def arrived(k, d, src, dst):
+        frm = lax.rem(me + nb - d, nb)
+        exchange(k, d, src, dst, frm, frm).wait_recv()
+        return frm
+
+    for q in range(nb):
+        at = pl.ds(q * rows, rows)
+        g = jax.nn.sigmoid(x_ref[at].astype(F32))
+        gate[q] = g
+        dz[q] = (cot_ref[at].astype(F32) * g).astype(BF16)
+    pl.semaphore_wait(barrier, nb - 1 + dp - 1)
+    push(0, dz, dz_in)
+
+    half = size // 2
+    for p in range(2):
+        part = jnp.dot(b_ref[p * half : (p + 1) * half], x_ref[...], preferred_element_type=F32)
+        h[p * nb // 2 : (p + 1) * nb // 2] = part.astype(BF16).reshape(nb // 2, rows, chan)
+    push(1, h, h_in)
+
+    i0 = lax.broadcasted_iota(jnp.int32, (side, side), 0)
+    i1 = lax.broadcasted_iota(jnp.int32, (side, side), 1)
+    to_ar = jnp.where(
+        (lax.rem(i0, group) == lax.div(i1, nb)) & (lax.div(i0, group) == lax.rem(i1, nb)), 1.0, 0.0
+    ).astype(BF16)
+    to_ra = jnp.where(
+        (lax.rem(i1, group) == lax.div(i0, nb)) & (lax.div(i1, group) == lax.rem(i0, nb)), 1.0, 0.0
+    ).astype(BF16)
+    same = lax.rem(i0, group) == lax.rem(i1, group)
+    e0 = lax.broadcasted_iota(jnp.int32, (nb, side), 0)
+    e1 = lax.broadcasted_iota(jnp.int32, (nb, side), 1)
+    spread = jnp.where(e0 == lax.div(e1, group), 1.0, 0.0).astype(BF16)
+    w_all = w_ref[...].astype(F32)
+    for g in range(groups):
+        flat = w_all[g * group : (g + 1) * group].reshape(side, nb).astype(BF16)
+        by_a = jnp.dot(to_ar, flat, preferred_element_type=F32).astype(BF16)
+        wide = jnp.dot(by_a, spread, preferred_element_type=F32)
+        weight[g] = jnp.where(same, wide, 0.0).astype(BF16)
+
+    for d in order:
+        arrived(0, d, dz, dz_in)
+    for g in range(groups):
+        at = pl.ds(g * group, group)
+        part = lax.dot_general(
+            weight[g], dz_in[:, at, :].reshape(side, chan), (((0,), (0,)), ((), ())),
+            preferred_element_type=F32,
+        )
+        dh_out[:, at, :] = part.astype(BF16).reshape(nb, group, chan)
+    push(2, dh_out, dh)
+
+    for d in order:
+        arrived(1, d, h, h_in)
+    for g in range(groups):
+        at = pl.ds(g * group, group)
+        part = jnp.dot(
+            weight[g], h_in[:, at, :].reshape(side, chan), preferred_element_type=F32
+        )
+        z_out[:, at, :] = part.astype(BF16).reshape(nb, group, chan)
+    push(3, z_out, z)
+
+    for g in range(groups):
+        at = pl.ds(g * group, group)
+        pairs = lax.dot_general(
+            dz_in[:, at, :].reshape(side, chan), h_in[:, at, :].reshape(side, chan),
+            (((1,), (1,)), ((), ())), preferred_element_type=F32,
+        )
+        kept = jnp.where(same, pairs, 0.0).astype(BF16)
+        picked = lax.dot_general(
+            spread, kept, (((1,), (1,)), ((), ())), preferred_element_type=F32
+        )
+        padded = jnp.concatenate([picked, jnp.zeros_like(picked)], axis=0)
+        cpart[:, g * side : (g + 1) * side] = padded.astype(BF16)
+
+    def share_cross(e, to, slot):
+        return pltpu.make_async_remote_copy(
+            src_ref=cpart,
+            dst_ref=crecv.at[slot],
+            send_sem=csend.at[e],
+            recv_sem=crecv_sem.at[e],
+            device_id={"dp": to},
+            device_id_type=MESH,
+        )
+
+    for e in range(1, dp):
+        share_cross(e, lax.rem(mp + e, dp), mp).start()
+    crecv[mp] = cpart[...]
+
+    for d in order:
+        arrived(2, d, dh_out, dh)
+    dh_all = dh[...].reshape(size, chan)
+    for p in range(dp):
+        part = lax.dot_general(
+            dh_all[p * share : (p + 1) * share], x_ref[...], (((1,), (1,)), ((), ())),
+            preferred_element_type=F32,
+        )
+        bpart[p] = part.astype(BF16)
+
+    def scatter(e, to, slot):
+        return pltpu.make_async_remote_copy(
+            src_ref=bpart.at[to],
+            dst_ref=brecv.at[slot],
+            send_sem=rsend.at[e],
+            recv_sem=rrecv.at[e],
+            device_id={"dp": to},
+            device_id_type=MESH,
+        )
+
+    for e in range(1, dp):
+        scatter(e, lax.rem(mp + e, dp), mp).start()
+    brecv[mp] = bpart[mp]
+
+    third = chan // 3
+    for p in range(3):
+        at = slice(p * third, (p + 1) * third)
+        dv[:, at] = lax.dot_general(
+            b_ref[...], dh_all[:, at], (((0,), (0,)), ((), ())), preferred_element_type=F32
+        )
+
+    for e in range(1, dp):
+        frm = lax.rem(mp + dp - e, dp)
+        share_cross(e, frm, frm).wait_recv()
+    total = crecv[0].astype(F32)
+    for p in range(1, dp):
+        total = total + crecv[p].astype(F32)
+    total = total[:nb].astype(BF16)
+    for g in range(groups):
+        mine = lax.dot_general(
+            to_ra, total[:, g * side : (g + 1) * side], (((1,), (1,)), ((), ())),
+            preferred_element_type=F32,
+        )
+        cg_ref[g * group : (g + 1) * group] = mine.reshape(group, nb, nb).astype(cg_ref.dtype)
+
+    for e in range(1, dp):
+        frm = lax.rem(mp + dp - e, dp)
+        scatter(e, frm, frm).wait_recv()
+    summed = brecv[0].astype(F32)
+    for p in range(1, dp):
+        summed = summed + brecv[p].astype(F32)
+    bg_ref[mp] = summed.astype(BF16)
+
+    def gather(e, to, slot):
+        return pltpu.make_async_remote_copy(
+            src_ref=bg_ref.at[slot],
+            dst_ref=bg_ref.at[slot],
+            send_sem=gsend.at[e],
+            recv_sem=grecv.at[e],
+            device_id={"dp": to},
+            device_id_type=MESH,
+        )
+
+    for e in range(1, dp):
+        gather(e, lax.rem(mp + e, dp), mp).start()
+
+    def finish(q):
+        at = pl.ds(pl.multiple_of(q * rows, rows), rows)
+        g = gate[q]
+        zg = z[q].astype(F32) * g
+        out_ref[at] = (x_ref[at].astype(F32) + zg).astype(BF16)
+        ig_ref[at] = (
+            cot_ref[at].astype(F32) * (1.0 + zg * (1.0 - g)) + dv[at]
+        ).astype(BF16)
+
+    finish(me)
+    for d in order:
+        finish(arrived(3, d, z_out, z))
+
+    for e in range(1, dp):
+        frm = lax.rem(mp + dp - e, dp)
+        gather(e, frm, frm).wait_recv()
+    for k, (src, dst) in enumerate(((dz, dz_in), (h, h_in), (dh_out, dh), (z_out, z))):
+        for d in order:
+            exchange(k, d, src, dst, lax.rem(me + d, nb), me).wait_send()
+    for e in range(1, dp):
+        to = lax.rem(mp + e, dp)
+        share_cross(e, to, mp).wait_send()
+        scatter(e, to, mp).wait_send()
+        gather(e, to, mp).wait_send()
+
+
+def fused(nb, dp, inputs, block_mix, cross_mix, cotangent):
+    _, size, chan = inputs.shape
+    rows = cross_mix.shape[0]
+    group = 256 // nb
+    side = nb * group
+    groups = rows // group
+    share = size // dp
+    act = (nb, rows, chan)
+    dma = pltpu.SemaphoreType.DMA
+    flops = 6 * size * size * chan + 6 * side * side * chan * groups
+    out, grad, block, cross = pl.pallas_call(
+        functools.partial(mix, nb, dp, rows, group),
+        out_shape=(
+            jax.ShapeDtypeStruct((size, chan), BF16),
+            jax.ShapeDtypeStruct((size, chan), BF16),
+            jax.ShapeDtypeStruct((dp, share, size), BF16),
+            jax.ShapeDtypeStruct((rows, nb, nb), BF16),
+        ),
+        in_specs=[pl.BlockSpec(memory_space=pltpu.VMEM)] * 4,
+        out_specs=(pl.BlockSpec(memory_space=pltpu.VMEM),) * 4,
+        scratch_shapes=[
+            pltpu.VMEM(act, F32),
+            *[pltpu.VMEM(act, BF16)] * 8,
+            pltpu.VMEM((size, chan), F32),
+            pltpu.VMEM((groups, side, side), BF16),
+            pltpu.VMEM((dp, share, size), BF16),
+            pltpu.VMEM((dp, share, size), BF16),
+            pltpu.VMEM((2 * nb, rows * nb), BF16),
+            pltpu.VMEM((dp, 2 * nb, rows * nb), BF16),
+            dma((4, nb)),
+            dma((4, nb)),
+            *[dma((dp,))] * 6,
+        ],
+        compiler_params=pltpu.CompilerParams(
+            collective_id=0, has_side_effects=True, vmem_limit_bytes=40 * 2**20
+        ),
+        cost_estimate=pl.CostEstimate(
+            flops=flops, bytes_accessed=8 * size * chan, transcendentals=size * chan
+        ),
+    )(inputs.reshape(size, chan), block_mix.reshape(size, size), cross_mix,
+      cotangent.reshape(size, chan))
+    return (
+        out.reshape(inputs.shape),
+        grad.reshape(inputs.shape),
+        block.reshape(block_mix.shape),
+        cross,
+    )
+
+
 def solution(mesh):
     placed = (
         P("dp", "seq", None),
@@ -42,6 +316,14 @@
         P("seq", None, None),
         P("dp", "seq", None),
     )
+    nb, dp = mesh.shape["seq"], mesh.shape["dp"]
+
+    def local(inputs, block_mix, cross_mix, cotangent):
+        rows = cross_mix.shape[0]
+        if nb in (8, 16) and rows % (256 // nb) == 0:
+            return fused(nb, dp, inputs, block_mix, cross_mix, cotangent)
+        return plain(inputs, block_mix, cross_mix, cotangent)
+
     return jax.shard_map(
         local,
         mesh=mesh,

time: 191 us -> 87.7 us (0.46)
  the two profiles are of different devices: /device:TPU:0 before, /device:TPU:13 now
where the time goes in v1:
time: 87.7 us; the launch traced here: 87.4 us
  Pallas kernels  79.3 us (90%)
  local copies, waits for them, and re-layouts  7.43 us (8%)
    pallas_call x1, Pallas kernels, fused(): pl.pallas_call(functools.partial(mix, nb, dp, rows, group), out_shape=(ja...  79.3 us
    unnamed x11, local copies, waits for them, and re-layouts  7.43 us

profile of v1, /device:TPU:13, one launch (start us, length us, event | category | flops | bytes accessed | tf_op | source)
XLA Modules:
  0.0 87.4 jit_solution(10110309165292505567)
XLA Ops:
  0.6 0.8 copy.8.w_ref
  1.5 0.0 copy-start
  1.5 1.1 %copy-done = bf16[1,512,768]{2,1,0:T(8,128)(2,1)S(1)} copy-done((bf16[1,512,768]{2,1,0:T(8,128)(2,1)S(1)}, bf16[1,512,768]{2,1,0:T(8,128)(2,1)}, u32[]{:S(2)}) %copy-start) | copy-done | bytes 786456
  2.6 0.0 copy-start.1
  2.6 1.1 %copy-done.1 = bf16[1,512,768]{2,1,0:T(8,128)(2,1)S(1)} copy-done((bf16[1,512,768]{2,1,0:T(8,128)(2,1)S(1)}, bf16[1,512,768]{2,1,0:T(8,128)(2,1)}, u32[]{:S(2)}) %copy-start.1) | copy-done | bytes 786456
  3.8 0.0 copy-start.2
  3.8 1.0 %copy-done.2 = bf16[1,512,512]{2,1,0:T(8,128)(2,1)S(1)} copy-done((bf16[1,512,512]{2,1,0:T(8,128)(2,1)S(1)}, bf16[1,512,512]{2,1,0:T(8,128)(2,1)}, u32[]{:S(2)}) %copy-start.2) | copy-done | bytes 524312
  4.8 79.3 %shard_map.75 = (bf16[512,768]{1,0:T(8,128)(2,1)S(1)}, bf16[512,768]{1,0:T(8,128)(2,1)S(1)}, bf16[4,128,512]{2,1,0:T(8,128)(2,1)S(1)}, bf16[64,8,8]{2,1,0:T(8,128)(2,1)S(1)}) custom-call(bf16[512,768]{1,0:T(8,128)(2,1)S(1)} %bitcast.9, bf16[512,512]{1,0:T(8,128)(2,1)S(1)} %bitcast.11, bf16[64,8,8]{2,1,0:T(8,128)(2,1)S(1)} %copy.8.w_ref, ...), custom_call_target="tpu_custom_call" | custom-call | flops 1811939328 | bytes 3145728 | tf_op jit(solution)/shard_map/pallas_call | solution.py:273
  84.1 0.7 copy.9
  84.8 0.9 %copy.13 = bf16[1,512,768]{2,1,0:T(8,128)(2,1)} copy(bf16[1,512,768]{2,1,0:T(8,128)(2,1)S(1)} %bitcast.7) | data formatting | bytes 1572864
  85.7 0.9 %copy.14 = bf16[1,512,768]{2,1,0:T(8,128)(2,1)} copy(bf16[1,512,768]{2,1,0:T(8,128)(2,1)S(1)} %bitcast.6) | data formatting | bytes 1572864
  86.6 0.8 copy.15
Async XLA Ops:
  1.5 1.1 %copy-start = (bf16[1,512,768]{2,1,0:T(8,128)(2,1)S(1)}, bf16[1,512,768]{2,1,0:T(8,128)(2,1)}, u32[]{:S(2)}) copy-start(bf16[1,512,768]{2,1,0:T(8,128)(2,1)} %param.4) | copy-start | bytes 2359300
  2.6 1.1 %copy-start.1 = (bf16[1,512,768]{2,1,0:T(8,128)(2,1)S(1)}, bf16[1,512,768]{2,1,0:T(8,128)(2,1)}, u32[]{:S(2)}) copy-start(bf16[1,512,768]{2,1,0:T(8,128)(2,1)} %param.7) | copy-start | bytes 2359300
  3.8 1.0 %copy-start.2 = (bf16[1,512,512]{2,1,0:T(8,128)(2,1)S(1)}, bf16[1,512,512]{2,1,0:T(8,128)(2,1)}, u32[]{:S(2)}) copy-start(bf16[1,512,512]{2,1,0:T(8,128)(2,1)} %param.5) | copy-start | bytes 1572868

commit v2 on v0

--- a/solution.py
+++ b/solution.py
@@ -1,10 +1,18 @@
+import functools
+
 import jax
 import jax.numpy as jnp
 from jax import lax
+from jax.experimental import pallas as pl
+from jax.experimental.pallas import tpu as pltpu
 from jax.sharding import PartitionSpec as P
 
-
-def local(inputs, block_mix, cross_mix, cotangent):
+MESH = pl.DeviceIdType.MESH
+BF16, F32 = jnp.bfloat16, jnp.float32
+VMEM_LIMIT = 63 * 2**20
+
+
+def plain(inputs, block_mix, cross_mix, cotangent):
     h = jnp.einsum("bsr,brc->bsc", block_mix, inputs, preferred_element_type=jnp.float32).astype(
         jnp.bfloat16
     )
@@ -35,6 +43,385 @@
     return (output, input_grad, block_sum.astype(jnp.bfloat16), cross_sum.astype(jnp.bfloat16))
 
 
+def mix(
+    nb, dp, rows, group,
+    x_hbm, b_hbm, w_ref, cot_hbm,
+    out_hbm, ig_hbm, bg_hbm, cg_hbm,
+    out_ref, ig_ref, bg_ref, cg_ref, x_ref, b_ref, cot_ref, gate, dz, h, dz_in, h_in, dh_out, z_out, dh, z, dv,
+    weight, bpart, bsum, brecv, cpart, crecv,
+    load, keep, send, recv, csend, crecv_sem, rsend, rrecv,
+):
+    me, mp = lax.axis_index("seq"), lax.axis_index("dp")
+    side = nb * group
+    groups = rows // group
+    size, chan = x_ref.shape
+    share = size // 4
+    order = range(nb - 1, 0, -1)
+
+    def partner(d):
+        to, bit = 0, 1
+        while bit < nb:
+            to = to + bit * lax.rem(lax.div(me, bit) + (d // bit) % 2, 2)
+            bit *= 2
+        return to
+
+    partners = {d: partner(d) for d in range(1, nb)}
+
+    def span(q):
+        return pl.ds(pl.multiple_of(q * rows, rows), rows)
+
+    def loads(d, q):
+        return (
+            pltpu.make_async_copy(x_hbm.at[span(q)], x_ref.at[span(q)], load.at[0, d]),
+            pltpu.make_async_copy(cot_hbm.at[span(q)], cot_ref.at[span(q)], load.at[1, d]),
+        )
+
+    barrier = pltpu.get_barrier_semaphore()
+    for d in order:
+        pl.semaphore_signal(
+            barrier, inc=1, device_id={"seq": partners[d]}, device_id_type=MESH
+        )
+    for e in range(1, dp):
+        pl.semaphore_signal(
+            barrier, inc=1, device_id={"dp": lax.rem(mp + e, dp)}, device_id_type=MESH
+        )
+    everyone = [*((d, partners[d]) for d in order), (0, me)]
+    for d, q in everyone:
+        for copy in loads(d, q):
+            copy.start()
+    b_copy = pltpu.make_async_copy(b_hbm, b_ref, load.at[2, 0])
+    b_copy.start()
+
+    def exchange(k, d, src, dst, slot):
+        return pltpu.make_async_remote_copy(
+            src_ref=src.at[partners[d]],
+            dst_ref=dst.at[slot],
+            send_sem=send.at[k, d],
+            recv_sem=recv.at[k, d],
+            device_id={"seq": partners[d]},
+            device_id_type=MESH,
+        )
+
+    buffers = ((dz, dz_in), (h, h_in), (dh_out, dh), (z_out, z))
+
+    def push(k):
+        for d in order:
+            exchange(k, d, *buffers[k], me).start()
+
+    def arrived(k, d):
+        exchange(k, d, *buffers[k], partners[d]).wait_recv()
+
+    for d, q in everyone:
+        for copy in loads(d, q):
+            copy.wait()
+        g = jax.nn.sigmoid(x_ref[span(q)].astype(F32))
+        gate[q] = g
+        part = (cot_ref[span(q)].astype(F32) * g).astype(BF16)
+        if d:
+            dz[q] = part
+            if d == nb - 1:
+                pl.semaphore_wait(barrier, nb - 1 + dp - 1)
+            exchange(0, d, dz, dz_in, me).start()
+        else:
+            dz_in[q] = part
+
+    b_copy.wait()
+    half = size // 2
+    for p in range(2):
+        part = jnp.dot(b_ref[p * half : (p + 1) * half], x_ref[...], preferred_element_type=F32)
+        h[p * nb // 2 : (p + 1) * nb // 2] = part.astype(BF16).reshape(nb // 2, rows, chan)
+    h_in[me] = h[me]
+
+    i0 = lax.broadcasted_iota(jnp.int32, (side, side), 0)
+    i1 = lax.broadcasted_iota(jnp.int32, (side, side), 1)
+    same = lax.rem(i0, group) == lax.rem(i1, group)
+    e0 = lax.broadcasted_iota(jnp.int32, (nb, side), 0)
+    e1 = lax.broadcasted_iota(jnp.int32, (nb, side), 1)
+    spread = jnp.where(e0 == lax.div(e1, group), 1.0, 0.0).astype(BF16)
+    w_all = w_ref[...].astype(F32)
+    for g in range(groups):
+        lanes = jnp.concatenate(
+            [w_all[:, b, g * group : (g + 1) * group] for b in range(nb)], axis=1
+        ).astype(BF16)
+        wide = lax.dot_general(
+            spread, lanes, (((0,), (0,)), ((), ())), preferred_element_type=F32
+        )
+        weight[g] = jnp.where(same, wide, 0.0).astype(BF16)
+    push(1)
+
+    for d in order:
+        arrived(0, d)
+    for g in range(groups):
+        at = pl.ds(g * group, group)
+        part = lax.dot_general(
+            weight[g], dz_in[:, at, :].reshape(side, chan), (((0,), (0,)), ((), ())),
+            preferred_element_type=F32,
+        )
+        dh_out[:, at, :] = part.astype(BF16).reshape(nb, group, chan)
+    dh[me] = dh_out[me]
+    push(2)
+
+    for d in order:
+        arrived(1, d)
+    for g in range(groups):
+        at = pl.ds(g * group, group)
+        part = jnp.dot(
+            weight[g], h_in[:, at, :].reshape(side, chan), preferred_element_type=F32
+        )
+        z_out[:, at, :] = part.astype(BF16).reshape(nb, group, chan)
+    z[me] = z_out[me]
+
+    def share_cross(e, to, slot):
+        return pltpu.make_async_remote_copy(
+            src_ref=cpart,
+            dst_ref=crecv.at[slot],
+            send_sem=csend.at[e],
+            recv_sem=crecv_sem.at[e],
+            device_id={"dp": to},
+            device_id_type=MESH,
+        )
+
+    def cross():
+        for g in range(groups):
+            at = pl.ds(g * group, group)
+            pairs = lax.dot_general(
+                dz_in[:, at, :].reshape(side, chan), h_in[:, at, :].reshape(side, chan),
+                (((1,), (1,)), ((), ())), preferred_element_type=F32,
+            )
+            kept = jnp.where(same, pairs, 0.0).astype(BF16)
+            picked = lax.dot_general(
+                spread, kept, (((1,), (1,)), ((), ())), preferred_element_type=F32
+            )
+            padded = jnp.concatenate([picked, jnp.zeros_like(picked)], axis=0)
+            cpart[:, g * side : (g + 1) * side] = padded.astype(BF16)
+        for e in range(1, dp):
+            share_cross(e, lax.rem(mp + e, dp), mp).start()
+        crecv[mp] = cpart[...]
+
+    push(3)
+
+    core = lax.rem(mp, 2)
+    by_core, by_x = mp + 1 - 2 * core, lax.rem(mp + 2, dp)
+    top = nb // 2
+    own = lax.div(me, top)
+
+    def hop(stage, p, src, dst, to):
+        return pltpu.make_async_remote_copy(
+            src_ref=src,
+            dst_ref=dst,
+            send_sem=rsend.at[stage, p],
+            recv_sem=rrecv.at[stage, p],
+            device_id={"dp": to},
+            device_id_type=MESH,
+        )
+
+    def hops(p, u):
+        return (
+            hop(0, p, bpart.at[p, 1 - core], brecv.at[0, p], by_core),
+            hop(1, p, bsum.at[p], brecv.at[1, p], by_x),
+            hop(2, p, bg_ref.at[u, core], bg_ref.at[u, core], by_core),
+        )
+
+    halves = tuple((p, u, hops(p, u)) for p, u in ((0, own), (1, 1 - own)))
+
+    def half_block(p, u, hop):
+        for d in order:
+            if (d >= top) == (p == 1):
+                arrived(2, d)
+        mine = dh[pl.ds(pl.multiple_of(u * top, top), top)].reshape(half, chan)
+        part = lax.dot_general(
+            mine, x_ref[...], (((1,), (1,)), ((), ())), preferred_element_type=F32
+        )
+        bpart[p] = part.astype(BF16).reshape(2, share, size)
+        hop[0].start()
+        at = pl.ds(pl.multiple_of(u * half, half), half)
+        third = chan // 3
+        for c in range(3):
+            cols = slice(c * third, (c + 1) * third)
+            value = lax.dot_general(
+                b_ref[at], mine[:, cols], (((0,), (0,)), ((), ())), preferred_element_type=F32
+            )
+            dv[:, cols] = value if p == 0 else dv[:, cols] + value
+
+    def pair_sum(p, u, hop):
+        hop[0].wait_recv()
+        bsum[p] = (bpart[p, core].astype(F32) + brecv[0, p].astype(F32)).astype(BF16)
+        hop[1].start()
+
+    def full_sum(p, u, hop):
+        hop[1].wait_recv()
+        bg_ref[u, core] = (bsum[p].astype(F32) + brecv[1, p].astype(F32)).astype(BF16)
+        hop[2].start()
+        keep_block(p, 0, u, core).start()
+
+    def keep_block(p, side, u, c):
+        return pltpu.make_async_copy(bg_ref.at[u, c], bg_hbm.at[u, c], keep.at[2, 2 * p + side])
+
+    half_block(*halves[0])
+    pair_sum(*halves[0])
+    cross()
+    half_block(*halves[1])
+    pair_sum(*halves[1])
+    full_sum(*halves[0])
+
+    for e in range(1, dp):
+        frm = lax.rem(mp + dp - e, dp)
+        share_cross(e, frm, frm).wait_recv()
+    total = crecv[0].astype(F32)
+    for p in range(1, dp):
+        total = total + crecv[p].astype(F32)
+    for a in range(nb):
+        cg_ref[a] = jnp.concatenate(
+            [
+                total[:nb, g * side + a * group : g * side + (a + 1) * group]
+                for g in range(groups)
+            ],
+            axis=1,
+        ).astype(BF16)
+    cg_copy = pltpu.make_async_copy(cg_ref, cg_hbm, keep.at[3, 0])
+    cg_copy.start()
+
+    def keep_rows(d, q):
+        return (
+            pltpu.make_async_copy(out_ref.at[span(q)], out_hbm.at[span(q)], keep.at[0, d]),
+            pltpu.make_async_copy(ig_ref.at[span(q)], ig_hbm.at[span(q)], keep.at[1, d]),
+        )
+
+    def finish(d, q):
+        at = span(q)
+        g = gate[q]
+        zg = z[q].astype(F32) * g
+        out_ref[at] = (x_ref[at].astype(F32) + zg).astype(BF16)
+        ig_ref[at] = (
+            cot_ref[at].astype(F32) * (1.0 + zg * (1.0 - g)) + dv[at]
+        ).astype(BF16)
+        for copy in keep_rows(d, q):
+            copy.start()
+
+    finish(0, me)
+    for d in order:
+        if d < top:
+            arrived(3, d)
+            finish(d, partners[d])
+    full_sum(*halves[1])
+    for d in order:
+        if d >= top:
+            arrived(3, d)
+            finish(d, partners[d])
+
+    for p, u, _ in halves:
+        hop(2, p, bg_ref.at[u, 1 - core], bg_ref.at[u, 1 - core], by_core).wait_recv()
+        keep_block(p, 1, u, 1 - core).start()
+    for k in range(4):
+        for d in order:
+            exchange(k, d, *buffers[k], me).wait_send()
+    for e in range(1, dp):
+        to = lax.rem(mp + e, dp)
+        share_cross(e, to, mp).wait_send()
+    for p, u, hop in halves:
+        for stage in hop:
+            stage.wait_send()
+        keep_block(p, 0, u, core).wait()
+        keep_block(p, 1, u, 1 - core).wait()
+    cg_copy.wait()
+    for d, q in everyone:
+        for copy in keep_rows(d, q):
+            copy.wait()
+
+
+def store(out, grad, block, cross, out_to, grad_to, block_to, cross_to, *rest):
+    *via, sems = rest
+    copies = []
+    arrays = ((out, out_to), (grad, grad_to), (block, block_to), (cross, cross_to))
+    for i, (src, dst) in enumerate(arrays):
+        pieces = 4 if i < 3 else 1
+        part = src.shape[0] // pieces
+        for p in range(pieces):
+            at = pl.ds(p * part, part)
+            copies.append((
+                pltpu.make_async_copy(src.at[at], via[i].at[at], sems.at[0, i, p]),
+                pltpu.make_async_copy(via[i].at[at], dst.at[at], sems.at[1, i, p]),
+            ))
+    for load, _ in copies:
+        load.start()
+    for load, keep in copies:
+        load.wait()
+        keep.start()
+    for _, keep in copies:
+        keep.wait()
+
+
+def fused(nb, dp, inputs, block_mix, cross_mix, cotangent):
+    _, size, chan = inputs.shape
+    rows = cross_mix.shape[0]
+    group = 256 // nb
+    side = nb * group
+    groups = rows // group
+    share = size // 4
+    act = (nb, rows, chan)
+    dma = pltpu.SemaphoreType.DMA
+    flops = 6 * size * size * chan + 6 * side * side * chan * groups
+    vmem, hbm = pl.BlockSpec(memory_space=pltpu.VMEM), pl.BlockSpec(memory_space=pltpu.HBM)
+    shapes = (
+        jax.ShapeDtypeStruct((size, chan), BF16),
+        jax.ShapeDtypeStruct((size, chan), BF16),
+        jax.ShapeDtypeStruct((2, 2, share, size), BF16),
+        jax.ShapeDtypeStruct((nb, nb, rows), BF16),
+    )
+    results = pl.pallas_call(
+        functools.partial(mix, nb, dp, rows, group),
+        out_shape=shapes,
+        in_specs=[hbm, hbm, vmem, hbm],
+        out_specs=(hbm,) * 4,
+        scratch_shapes=[
+            pltpu.VMEM((size, chan), BF16),
+            pltpu.VMEM((size, chan), BF16),
+            pltpu.VMEM((2, 2, share, size), BF16),
+            pltpu.VMEM((nb, nb, rows), BF16),
+            pltpu.VMEM((size, chan), BF16),
+            pltpu.VMEM((size, size), BF16),
+            pltpu.VMEM((size, chan), BF16),
+            pltpu.VMEM(act, F32),
+            *[pltpu.VMEM(act, BF16)] * 8,
+            pltpu.VMEM((size, chan), F32),
+            pltpu.VMEM((groups, side, side), BF16),
+            pltpu.VMEM((2, 2, share, size), BF16),
+            pltpu.VMEM((2, share, size), BF16),
+            pltpu.VMEM((2, 2, share, size), BF16),
+            pltpu.VMEM((2 * nb, rows * nb), BF16),
+            pltpu.VMEM((dp, 2 * nb, rows * nb), BF16),
+            dma((3, nb)),
+            dma((4, max(nb, dp))),
+            dma((4, nb)),
+            dma((4, nb)),
+            *[dma((dp,))] * 2,
+            *[dma((3, 2))] * 2,
+        ],
+        compiler_params=pltpu.CompilerParams(
+            collective_id=0, has_side_effects=True, vmem_limit_bytes=VMEM_LIMIT
+        ),
+        cost_estimate=pl.CostEstimate(
+            flops=flops, bytes_accessed=8 * size * chan, transcendentals=size * chan
+        ),
+    )(inputs.reshape(size, chan), block_mix.reshape(size, size),
+      cross_mix.transpose(1, 2, 0), cotangent.reshape(size, chan))
+    shapes = (*shapes[:2], jax.ShapeDtypeStruct((size, size), BF16), shapes[3])
+    out, grad, block, cross = pl.pallas_call(
+        store,
+        out_shape=shapes,
+        in_specs=[hbm] * 4,
+        out_specs=(hbm,) * 4,
+        scratch_shapes=[*[pltpu.VMEM(a.shape, BF16) for a in shapes], dma((2, 4, 4))],
+        compiler_params=pltpu.CompilerParams(vmem_limit_bytes=VMEM_LIMIT),
+    )(*results[:2], results[2].reshape(shapes[2].shape), results[3])
+    return (
+        out.reshape(inputs.shape),
+        grad.reshape(inputs.shape),
+        block.reshape(block_mix.shape),
+        cross.transpose(2, 0, 1),
+    )
+
+
 def solution(mesh):
     placed = (
         P("dp", "seq", None),
@@ -42,6 +429,14 @@
         P("seq", None, None),
         P("dp", "seq", None),
     )
+    nb, dp = mesh.shape["seq"], mesh.shape["dp"]
+
+    def local(inputs, block_mix, cross_mix, cotangent):
+        rows = cross_mix.shape[0]
+        if nb in (8, 16) and dp == 4 and rows % (256 // nb) == 0:
+            return fused(nb, dp, inputs, block_mix, cross_mix, cotangent)
+        return plain(inputs, block_mix, cross_mix, cotangent)
+
     return jax.shard_map(
         local,
         mesh=mesh,

time: 191 us -> 80.8 us (0.42)
  Pallas kernels: 0 us -> 79.9 us
  waiting for transfers between devices: 67.4 us -> 0 us
  blocking collectives: 36.1 us -> 0 us
  local copies, waits for them, and re-layouts: 29.5 us -> 0 us
  other arithmetic: 16.4 us -> 0 us
  starting transfers between devices: 15.5 us -> 0 us
  between operations: 14.2 us -> 0.64 us
  matrix products: 10.9 us -> 0 us
    pallas_call x0 -> x2, Pallas kernels: none -> 79.9 us  [the longest x1 77.3 us: fused(): pl.pallas_call(functools.partial(mix, nb, dp, rows, group), out_shape=sha...]
    all_to_all x3 -> x0, waiting for transfers between devices: 40.6 us -> none  [the longest x1 20 us: local(): h_cols = lax.all_to_all(h, 'seq', split_axis=1, concat_axis=0, tiled=True)]
    psum x1 -> x0, waiting for transfers between devices: 26.8 us -> none  [local(): lax.psum(block_part.astype(jnp.bfloat16), 'dp').astype(jnp.float32)]
    all_to_all x1 -> x0, blocking collectives: 23.8 us -> none  [local(): dz_cols = lax.all_to_all(dz, 'seq', split_axis=1, concat_axis=0, tiled=True)]
    unnamed x32 -> x0, local copies, waits for them, and re-layouts: 20.9 us -> none
    all_to_all x3 -> x0, starting transfers between devices: 15.5 us -> none  [the longest x1 7.28 us: local(): h_cols = lax.all_to_all(h, 'seq', split_axis=1, concat_axis=0, tiled=True)]
    psum x1 -> x0, blocking collectives: 12.4 us -> none  [local(): lax.psum(cross_part.astype(jnp.bfloat16), 'dp').astype(jnp.float32)]
    unnamed x2 -> x0, other arithmetic: 11.7 us -> none
  transfers between devices with their start and end apart: 4 -> 0, of which waited for: 4 -> 0; matrix products, arithmetic and copies ran while one was open for 6% -> 0% of each run, Pallas kernels for 0% -> 0%
where the time goes in v2:
time: 80.8 us; the launch traced here: 80.6 us
  Pallas kernels  79.9 us (99%)
    pallas_call x1, Pallas kernels, fused(): pl.pallas_call(functools.partial(mix, nb, dp, rows, group), out_shape=sha...  77.3 us
    pallas_call x1, Pallas kernels, fused(): pl.pallas_call(store, out_shape=shapes, in_specs=[hbm] * 4, out_specs=(hb...  2.61 us

profile of v2, /device:TPU:0, one launch (start us, length us, event | category | flops | bytes accessed | tf_op | source)
XLA Modules:
  0.0 80.6 jit_solution(4635679484308110564)
XLA Ops:
  0.6 77.3 %shard_map.75 = (bf16[512,768]{1,0:T(8,128)(2,1)}, bf16[512,768]{1,0:T(8,128)(2,1)}, bf16[2,2,128,512]{3,2,1,0:T(8,128)(2,1)}, bf16[8,8,64]{2,1,0:T(8,128)(2,1)}) custom-call(bf16[512,768]{1,0:T(8,128)(2,1)} %bitcast.10, bf16[512,512]{1,0:T(8,128)(2,1)} %bitcast.14, bf16[8,8,64]{2,1,0:T(8,128)(2,1)} %bitcast.16, bf16[512,768]{1,0:T(8,128)(2,1)} %bitcast.11), custom_call_target="tpu_custom_call" | custom-call | flops 1811939328 | bytes 3145728 | tf_op jit(solution)/shard_map/pallas_call | solution.py:371
  78.0 2.6 %shard_map.76 = (bf16[512,768]{1,0:T(8,128)(2,1)}, bf16[512,768]{1,0:T(8,128)(2,1)}, bf16[512,512]{1,0:T(8,128)(2,1)}, bf16[8,8,64]{2,1,0:T(8,128)(2,1)}) custom-call(bf16[512,768]{1,0:T(8,128)(2,1)} %get-tuple-element.12.out, bf16[512,768]{1,0:T(8,128)(2,1)} %get-tuple-element.13.grad, bf16[512,512]{1,0:T(8,128)(2,1)} %bitcast.9, ...), custom_call_target="tpu_custom_call" | custom-call | tf_op jit(solution)/shard_map/pallas_call | solution.py:409

commit v3 on v2

--- a/solution.py
+++ b/solution.py
@@ -9,7 +9,7 @@
 
 MESH = pl.DeviceIdType.MESH
 BF16, F32 = jnp.bfloat16, jnp.float32
-VMEM_LIMIT = 63 * 2**20
+VMEM_LIMIT = 51 * 2**20
 
 
 def plain(inputs, block_mix, cross_mix, cotangent):
@@ -46,10 +46,10 @@
 def mix(
     nb, dp, rows, group,
     x_hbm, b_hbm, w_ref, cot_hbm,
-    out_hbm, ig_hbm, bg_hbm, cg_hbm,
-    out_ref, ig_ref, bg_ref, cg_ref, x_ref, b_ref, cot_ref, gate, dz, h, dz_in, h_in, dh_out, z_out, dh, z, dv,
+    out_ref, ig_ref, bg_ref, cg_ref,
+    x_ref, b_ref, cot_ref, gate, dz, h, dz_in, h_in, dh_out, z_out, dh, z, dv,
     weight, bpart, bsum, brecv, cpart, crecv,
-    load, keep, send, recv, csend, crecv_sem, rsend, rrecv,
+    load, send, recv, csend, crecv_sem, rsend, rrecv,
 ):
     me, mp = lax.axis_index("seq"), lax.axis_index("dp")
     side = nb * group
@@ -252,10 +252,6 @@
         hop[1].wait_recv()
         bg_ref[u, core] = (bsum[p].astype(F32) + brecv[1, p].astype(F32)).astype(BF16)
         hop[2].start()
-        keep_block(p, 0, u, core).start()
-
-    def keep_block(p, side, u, c):
-        return pltpu.make_async_copy(bg_ref.at[u, c], bg_hbm.at[u, c], keep.at[2, 2 * p + side])
 
     half_block(*halves[0])
     pair_sum(*halves[0])
@@ -278,15 +274,6 @@
             ],
             axis=1,
         ).astype(BF16)
-    cg_copy = pltpu.make_async_copy(cg_ref, cg_hbm, keep.at[3, 0])
-    cg_copy.start()
-
-    def keep_rows(d, q):
-        return (
-            pltpu.make_async_copy(out_ref.at[span(q)], out_hbm.at[span(q)], keep.at[0, d]),
-            pltpu.make_async_copy(ig_ref.at[span(q)], ig_hbm.at[span(q)], keep.at[1, d]),
-        )
-
     def finish(d, q):
         at = span(q)
         g = gate[q]
@@ -295,8 +282,6 @@
         ig_ref[at] = (
             cot_ref[at].astype(F32) * (1.0 + zg * (1.0 - g)) + dv[at]
         ).astype(BF16)
-        for copy in keep_rows(d, q):
-            copy.start()
 
     finish(0, me)
     for d in order:
@@ -311,7 +296,6 @@
 
     for p, u, _ in halves:
         hop(2, p, bg_ref.at[u, 1 - core], bg_ref.at[u, 1 - core], by_core).wait_recv()
-        keep_block(p, 1, u, 1 - core).start()
     for k in range(4):
         for d in order:
             exchange(k, d, *buffers[k], me).wait_send()
@@ -321,16 +305,9 @@
     for p, u, hop in halves:
         for stage in hop:
             stage.wait_send()
-        keep_block(p, 0, u, core).wait()
-        keep_block(p, 1, u, 1 - core).wait()
-    cg_copy.wait()
-    for d, q in everyone:
-        for copy in keep_rows(d, q):
-            copy.wait()
-
-
-def store(out, grad, block, cross, out_to, grad_to, block_to, cross_to, *rest):
-    *via, sems = rest
+
+
+def store(out, grad, block, cross, out_to, grad_to, block_to, cross_to, sems):
     copies = []
     arrays = ((out, out_to), (grad, grad_to), (block, block_to), (cross, cross_to))
     for i, (src, dst) in enumerate(arrays):
@@ -338,17 +315,11 @@
         part = src.shape[0] // pieces
         for p in range(pieces):
             at = pl.ds(p * part, part)
-            copies.append((
-                pltpu.make_async_copy(src.at[at], via[i].at[at], sems.at[0, i, p]),
-                pltpu.make_async_copy(via[i].at[at], dst.at[at], sems.at[1, i, p]),
-            ))
-    for load, _ in copies:
-        load.start()
-    for load, keep in copies:
-        load.wait()
-        keep.start()
-    for _, keep in copies:
-        keep.wait()
+            copies.append(pltpu.make_async_copy(src.at[at], dst.at[at], sems.at[i, p]))
+    for copy in copies:
+        copy.start()
+    for copy in copies:
+        copy.wait()
 
 
 def fused(nb, dp, inputs, block_mix, cross_mix, cotangent):
@@ -372,12 +343,8 @@
         functools.partial(mix, nb, dp, rows, group),
         out_shape=shapes,
         in_specs=[hbm, hbm, vmem, hbm],
-        out_specs=(hbm,) * 4,
+        out_specs=(vmem,) * 4,
         scratch_shapes=[
-            pltpu.VMEM((size, chan), BF16),
-            pltpu.VMEM((size, chan), BF16),
-            pltpu.VMEM((2, 2, share, size), BF16),
-            pltpu.VMEM((nb, nb, rows), BF16),
             pltpu.VMEM((size, chan), BF16),
             pltpu.VMEM((size, size), BF16),
             pltpu.VMEM((size, chan), BF16),
@@ -391,7 +358,6 @@
             pltpu.VMEM((2 * nb, rows * nb), BF16),
             pltpu.VMEM((dp, 2 * nb, rows * nb), BF16),
             dma((3, nb)),
-            dma((4, max(nb, dp))),
             dma((4, nb)),
             dma((4, nb)),
             *[dma((dp,))] * 2,
@@ -409,10 +375,10 @@
     out, grad, block, cross = pl.pallas_call(
         store,
         out_shape=shapes,
-        in_specs=[hbm] * 4,
+        in_specs=[pl.BlockSpec(memory_space=pl.ANY)] * 4,
         out_specs=(hbm,) * 4,
-        scratch_shapes=[*[pltpu.VMEM(a.shape, BF16) for a in shapes], dma((2, 4, 4))],
-        compiler_params=pltpu.CompilerParams(vmem_limit_bytes=VMEM_LIMIT),
+        scratch_shapes=[dma((4, 4))],
+        compiler_params=pltpu.CompilerParams(vmem_limit_bytes=2**20),
     )(*results[:2], results[2].reshape(shapes[2].shape), results[3])
     return (
         out.reshape(inputs.shape),

time: 80.8 us -> 79.7 us (0.986)
  Pallas kernels: 79.9 us -> 77 us
  local copies, waits for them, and re-layouts: 0 us -> 1.75 us
    pallas_call x1, Pallas kernels: 77.3 us -> 75.6 us  [fused(): pl.pallas_call(functools.partial(mix, nb, dp, rows, group), out_shape=sha...]
    unnamed x0 -> x4, local copies, waits for them, and re-layouts: none -> 1.75 us
    pallas_call x1, Pallas kernels: 2.61 us -> 1.45 us  [fused(): pl.pallas_call(store, out_shape=shapes, in_specs=[pl.BlockSpec(memory_spa...]
where the time goes in v3:
time: 79.7 us; the launch traced here: 79.4 us
  Pallas kernels  77 us (97%)
  local copies, waits for them, and re-layouts  1.75 us (2%)
    pallas_call x1, Pallas kernels, fused(): pl.pallas_call(functools.partial(mix, nb, dp, rows, group), out_shape=sha...  75.6 us
    unnamed x4, local copies, waits for them, and re-layouts  1.75 us

profile of v3, /device:TPU:0, one launch (start us, length us, event | category | flops | bytes accessed | tf_op | source)
XLA Modules:
  0.0 79.4 jit_solution(11299211277780798326)
XLA Ops:
  0.6 0.0 copy-start
  0.6 1.0 %copy-done = bf16[1,512,512]{2,1,0:T(8,128)(2,1)S(1)} copy-done((bf16[1,512,512]{2,1,0:T(8,128)(2,1)S(1)}, bf16[1,512,512]{2,1,0:T(8,128)(2,1)}, u32[]{:S(2)}) %copy-start) | copy-done | bytes 524312
  1.7 0.0 copy-start.1
  1.7 0.7 copy-done.1
  2.4 75.6 %shard_map.75 = (bf16[512,768]{1,0:T(8,128)(2,1)S(1)}, bf16[512,768]{1,0:T(8,128)(2,1)S(1)}, bf16[2,2,128,512]{3,2,1,0:T(8,128)(2,1)S(1)}, bf16[8,8,64]{2,1,0:T(8,128)(2,1)S(1)}) custom-call(bf16[512,768]{1,0:T(8,128)(2,1)} %bitcast.12, bf16[512,512]{1,0:T(8,128)(2,1)S(1)} %bitcast.10, bf16[8,8,64]{2,1,0:T(8,128)(2,1)S(1)} %bitcast.11, bf16[512,768]{1,0:T(8,128)(2,1)} %bitcast.13), custom_call_target="tpu_custom_call" | custom-call | flops 1811939328 | bytes 3145728 | tf_op jit(solution)/shard_map/pallas_call | solution.py:342
  78.0 1.4 %shard_map.76 = (bf16[512,768]{1,0:T(8,128)(2,1)}, bf16[512,768]{1,0:T(8,128)(2,1)}, bf16[512,512]{1,0:T(8,128)(2,1)}, bf16[8,8,64]{2,1,0:T(8,128)(2,1)}) custom-call(bf16[512,768]{1,0:T(8,128)(2,1)S(1)} %get-tuple-element.12.out, bf16[512,768]{1,0:T(8,128)(2,1)S(1)} %get-tuple-element.13.grad, bf16[512,512]{1,0:T(8,128)(2,1)S(1)} %bitcast.9, ...), custom_call_target="tpu_custom_call" | custom-call | tf_op jit(solution)/shard_map/pallas_call | solution.py:375
Async XLA Ops:
  0.6 1.0 %copy-start = (bf16[1,512,512]{2,1,0:T(8,128)(2,1)S(1)}, bf16[1,512,512]{2,1,0:T(8,128)(2,1)}, u32[]{:S(2)}) copy-start(bf16[1,512,512]{2,1,0:T(8,128)(2,1)} %param.5) | copy-start | bytes 1572868
  1.7 0.7 copy-start.1

commit v4 on v3

--- a/solution.py
+++ b/solution.py
@@ -56,7 +56,8 @@
     groups = rows // group
     size, chan = x_ref.shape
     share = size // 4
-    order = range(nb - 1, 0, -1)
+    far = nb // 2
+    order = [*range(far + far // 2 - 1, far - 1, -1), *range(nb - 1, far + far // 2 - 1, -1), *range(far - 1, 0, -1)]
 
     def partner(d):
         to, bit = 0, 1
@@ -119,7 +120,7 @@
         part = (cot_ref[span(q)].astype(F32) * g).astype(BF16)
         if d:
             dz[q] = part
-            if d == nb - 1:
+            if d == order[0]:
                 pl.semaphore_wait(barrier, nb - 1 + dp - 1)
             exchange(0, d, dz, dz_in, me).start()
         else:

time: 79.7 us -> 77.7 us (0.975)
  the two profiles are of different devices: /device:TPU:0 before, /device:TPU:17 now
where the time goes in v4:
time: 77.7 us; the launch traced here: 77.4 us
  Pallas kernels  75 us (97%)
  local copies, waits for them, and re-layouts  1.75 us (2%)
    pallas_call x1, Pallas kernels, fused(): pl.pallas_call(functools.partial(mix, nb, dp, rows, group), out_shape=sha...  73.6 us
    unnamed x4, local copies, waits for them, and re-layouts  1.75 us

profile of v4, /device:TPU:17, one launch (start us, length us, event | category | flops | bytes accessed | tf_op | source)
XLA Modules:
  0.0 77.4 jit_solution(8771562231458783697)
XLA Ops:
  0.6 0.0 copy-start
  0.6 1.0 %copy-done = bf16[1,512,512]{2,1,0:T(8,128)(2,1)S(1)} copy-done((bf16[1,512,512]{2,1,0:T(8,128)(2,1)S(1)}, bf16[1,512,512]{2,1,0:T(8,128)(2,1)}, u32[]{:S(2)}) %copy-start) | copy-done | bytes 524312
  1.7 0.0 copy-start.1
  1.7 0.7 copy-done.1
  2.4 73.6 %shard_map.75 = (bf16[512,768]{1,0:T(8,128)(2,1)S(1)}, bf16[512,768]{1,0:T(8,128)(2,1)S(1)}, bf16[2,2,128,512]{3,2,1,0:T(8,128)(2,1)S(1)}, bf16[8,8,64]{2,1,0:T(8,128)(2,1)S(1)}) custom-call(bf16[512,768]{1,0:T(8,128)(2,1)} %bitcast.12, bf16[512,512]{1,0:T(8,128)(2,1)S(1)} %bitcast.10, bf16[8,8,64]{2,1,0:T(8,128)(2,1)S(1)} %bitcast.11, bf16[512,768]{1,0:T(8,128)(2,1)} %bitcast.13), custom_call_target="tpu_custom_call" | custom-call | flops 1811939328 | bytes 3145728 | tf_op jit(solution)/shard_map/pallas_call | solution.py:343
  76.0 1.4 %shard_map.76 = (bf16[512,768]{1,0:T(8,128)(2,1)}, bf16[512,768]{1,0:T(8,128)(2,1)}, bf16[512,512]{1,0:T(8,128)(2,1)}, bf16[8,8,64]{2,1,0:T(8,128)(2,1)}) custom-call(bf16[512,768]{1,0:T(8,128)(2,1)S(1)} %get-tuple-element.12.out, bf16[512,768]{1,0:T(8,128)(2,1)S(1)} %get-tuple-element.13.grad, bf16[512,512]{1,0:T(8,128)(2,1)S(1)} %bitcast.9, ...), custom_call_target="tpu_custom_call" | custom-call | tf_op jit(solution)/shard_map/pallas_call | solution.py:376
Async XLA Ops:
  0.6 1.0 %copy-start = (bf16[1,512,512]{2,1,0:T(8,128)(2,1)S(1)}, bf16[1,512,512]{2,1,0:T(8,128)(2,1)}, u32[]{:S(2)}) copy-start(bf16[1,512,512]{2,1,0:T(8,128)(2,1)} %param.5) | copy-start | bytes 1572868
  1.7 0.7 copy-start.1
